TPU v7x, 32 devices: a whole 2x2x4 slice. The times are simulated.
32 devices in a mesh: groups: 2 (over y), leaf: 8 (over z, x), sub: 2 (over core).
Axes of the slice: x: 2, y: 2, z: 4, core: 2. Of those that a mesh axis runs over, the one named last changes fastest.
Arguments:
- charges: float32 [32, 131072], P(None, ('groups', 'leaf', 'sub')), parts along dimension 1, may hold values from -6 to 6
- coords: float32 [3, 131072], P(None, ('groups', 'leaf', 'sub')), parts along dimension 1, may hold values from 0 to 1
- basis: bfloat16 [64, 131072], P(None, ('groups', 'leaf', 'sub')), parts along dimension 1, may hold values from -0.5 to 0.5
- near_offsets: int32 [27, 1024], P(None, ('groups', 'leaf', 'sub')), parts along dimension 1, may hold values from -16 to 16, as said below
- near_count: int32 [1024], P(('groups', 'leaf', 'sub')), parts along dimension 0, may hold values from 10 to 27
- transfer: float32 [7, 2, 64, 64], replicated, may hold values from -0.5 to 0.5
- coupling: float32 [8, 4, 64, 64], replicated, as said below
- far_used: int32 [4, 2040], P(None, 'groups'), parts along dimension 1, may hold values 0 or 1
Outputs:
- potentials: float32 [32, 131072], P(None, ('groups', 'leaf', 'sub')), parts along dimension 1
There are 2 independent parts, one for each index of `groups`. A program takes and returns all parts, laid end to end along the dimension named above; an argument that names none is the same for every part. Nothing has to cross between parts.
Inputs may be any that keep to these rules, and one draw needn't show every extreme that they name: `near_offsets`: slot 0 of every leaf is 0 (the leaf itself); the other slots of a leaf hold distinct nonzero offsets; a source leaf may lie outside the leaves, and then adds nothing. The first near_count[i] slots of leaf i are used. `coupling`: coupling tables of order one after the product with a node's coefficients.
All inputs are finite; a program needn't handle non-finite values.
Results may differ from a plain program's by a relative error of at most 0.004.
Values sent between devices are 32-bit elements; how exact they have to be, the bound alone decides.
A program may use at most 64 MiB of HBM per device.

v0:
```python
import jax
import jax.numpy as jnp
from jax import lax
from jax.sharding import PartitionSpec as P

decay_rate = 1.7320508075688772 / 0.15
far_offsets = (-3, -2, 2, 3)
highest = lax.Precision.HIGHEST


def shifted(x, axis, by):
    size = lax.axis_size(axis)
    pairs = [(i, i + by) for i in range(size) if 0 <= i + by < size]
    return lax.ppermute(x, axis, pairs)


def with_halo(x, sides, width):
    for axis, dim in sides:
        size, length = (lax.axis_size(axis), x.shape[dim])
        up = [(i, (i + 1) % size) for i in range(size - 1)]
        down = [(j, i) for i, j in up]
        last = lax.slice_in_dim(x, length - width, length, axis=dim)
        first = lax.slice_in_dim(x, 0, width, axis=dim)
        before = lax.ppermute(last, axis, up)
        after = lax.ppermute(first, axis, down)
        x = jnp.concatenate([before, x, after], axis=dim)
    return x


def swapped(value, axis, stride):
    mask = 2**stride
    pairs = [(source, source ^ mask) for source in range(lax.axis_size(axis))]
    return lax.ppermute(value, axis, pairs)


def matern(targets, spots):
    gap_x = targets[0] - spots[0]
    gap_y = targets[1] - spots[1]
    gap_z = targets[2] - spots[2]
    scaled = decay_rate * jnp.sqrt(gap_x * gap_x + gap_y * gap_y + gap_z * gap_z)
    return ((1.0 + scaled) * jnp.exp(-scaled)).astype(jnp.bfloat16)


def lift(lower, transfer, height):
    return jnp.einsum(
        "jk,njr->nkr", transfer[height, 0], lower[0::2], precision=highest
    ) + jnp.einsum("jk,njr->nkr", transfer[height, 1], lower[1::2], precision=highest)


def couple(window, start, count, table, flags):
    total = jnp.zeros((count,) + window.shape[1:], jnp.float32)
    for which, offset in enumerate(far_offsets):
        piece = window[start + offset : start + offset + count]
        term = jnp.einsum("kj,njr->nkr", table[which], piece, precision=highest)
        total = total + flags[which][:, None, None].astype(jnp.float32) * term
    return total


def edge_window(block):
    lower = shifted(block[-3:], ("leaf", "sub"), 1)
    upper = shifted(block[:3], ("leaf", "sub"), -1)
    return jnp.concatenate([lower, block, upper], axis=0)


def pair_window(block):
    below = [shifted(block, ("leaf", "sub"), spacing) for spacing in (2, 1)]
    above = [shifted(block, ("leaf", "sub"), -spacing) for spacing in (1, 2)]
    return jnp.concatenate(below + [block] + above, axis=0)


def tree_window(block, spacing):
    below = [shifted(block, ("leaf", "sub"), times * spacing) for times in (3, 2, 1)]
    above = [shifted(block, ("leaf", "sub"), -times * spacing) for times in (1, 2, 3)]
    return jnp.concatenate(below + [block] + above, axis=0)


def local(charges, coords, basis, near_offsets, near_count, transfer, coupling, far_used):
    leaf_count = near_count.shape[0]
    width = charges.shape[1]
    leaf_size = width // leaf_count
    columns = charges.shape[0]
    devices = lax.axis_size(("leaf", "sub"))
    position = lax.axis_index(("leaf", "sub"))
    dev_levels = leaf_count.bit_length() - 1
    summit = coupling.shape[0] - 1
    leaves = leaf_count * devices
    reach = leaf_count // 2
    packed = jnp.concatenate([charges, coords], axis=0)
    widened = with_halo(packed, ((("leaf", "sub"), 1),), reach * leaf_size)
    spanned = leaf_count + 2 * reach
    sources = widened[:columns].astype(jnp.bfloat16).reshape(columns, spanned, leaf_size)
    places = widened[columns:].reshape(3, spanned, leaf_size)
    group = max(1, leaf_count // 16)
    starts = jnp.arange(0, leaf_count, group, dtype=jnp.int32)
    slots = jnp.arange(near_offsets.shape[0], dtype=jnp.int32)

    def near_group(start):
        leaf_ids = start + jnp.arange(group, dtype=jnp.int32)
        offsets = lax.dynamic_slice_in_dim(near_offsets, start, group, 1)
        counts = lax.dynamic_slice_in_dim(near_count, start, group, 0)
        picks = (leaf_ids[None, :] + reach + offsets).T
        used = (slots[None, :] < counts[:, None]).astype(jnp.bfloat16)
        chosen = sources[:, picks] * used[None, :, :, None]
        spots = places[:, picks]
        targets = lax.dynamic_slice_in_dim(places, start + reach, group, 1)
        block = matern(targets[:, :, None, :, None], spots[:, :, :, None, :])
        return jnp.einsum("gspq,rgsq->rgp", block, chosen, preferred_element_type=jnp.float32)

    near_parts = lax.map(near_group, starts)
    near_part = near_parts.transpose(1, 0, 2, 3).reshape(columns, width)
    charges_low = charges.astype(jnp.bfloat16).reshape(columns, leaf_count, leaf_size)
    basis_leaf = basis.reshape(basis.shape[0], leaf_count, leaf_size)
    levels = [
        jnp.einsum("kns,rns->nkr", basis_leaf, charges_low, preferred_element_type=jnp.float32)
    ]
    for height in range(dev_levels):
        levels.append(lift(levels[-1], transfer, height))
    windows = {}
    for height in range(dev_levels - 1):
        windows[height] = (edge_window(levels[height]), 3)
    windows[dev_levels - 1] = (pair_window(levels[dev_levels - 1]), 4)
    node = levels[dev_levels]
    for step in range(summit - dev_levels + 1):
        windows[dev_levels + step] = (tree_window(node, 2**step), 3)
        if dev_levels + step < summit:
            other = swapped(node, ("leaf", "sub"), step)
            right = position // 2**step % 2 == 1
            first = jnp.where(right, other, node)
            second = jnp.where(right, node, other)
            node = lift(jnp.concatenate([first, second], axis=0), transfer, dev_levels + step)
    totals = None
    for height in range(summit, -1, -1):
        window, start = windows[height]
        count = max(1, leaf_count >> height)
        base = 2 * leaves - 2 * (leaves >> height)
        if height >= dev_levels:
            first_node = position // 2 ** (height - dev_levels)
        else:
            first_node = position * count
        flags = lax.dynamic_slice_in_dim(far_used, base + first_node, count, 1)
        own = couple(window, start, count, coupling[height], flags)
        if totals is None:
            totals = own
        elif height >= dev_levels:
            table = jnp.where(first_node % 2 == 0, transfer[height, 0], transfer[height, 1])
            totals = own + jnp.einsum("jk,nkr->njr", table, totals, precision=highest)
        else:
            first = jnp.einsum("jk,nkr->njr", transfer[height, 0], totals, precision=highest)
            second = jnp.einsum("jk,nkr->njr", transfer[height, 1], totals, precision=highest)
            totals = own + jnp.stack([first, second], 1).reshape(own.shape)
    leaf_coef = totals.astype(jnp.bfloat16)
    far_part = jnp.einsum(
        "kns,nkr->rns", basis_leaf, leaf_coef, preferred_element_type=jnp.float32
    ).reshape(columns, width)
    return far_part + near_part


def solution(mesh):
    in_specs = (
        P(None, ("groups", "leaf", "sub")),
        P(None, ("groups", "leaf", "sub")),
        P(None, ("groups", "leaf", "sub")),
        P(None, ("groups", "leaf", "sub")),
        P(("groups", "leaf", "sub")),
        P(),
        P(),
        P(None, "groups"),
    )
    out_specs = P(None, ("groups", "leaf", "sub"))
    return jax.shard_map(local, mesh=mesh, in_specs=in_specs, out_specs=out_specs, check_vma=False)
```

profile of v0, /device:TPU:11, one launch (start us, length us, event | category | flops | bytes accessed | tf_op | source)
XLA Modules:
  0.0 308.4 jit_solution(7541654358665165757)
XLA Ops:
  8.8 3.9 %collective-permute-start.9 = (f32[2,64,32]{1,2,0:T(8,128)S(1)}, f32[2,64,32]{1,2,0:T(8,128)}, u32[]{:S(2)}, u32[]{:S(2)}) collective-permute-start(f32[2,64,32]{1,2,0:T(8,128)S(1)} %fusion.41), channel_id=1, source_target_pairs={{0,1},{1,2},{2,3},{3,4},{4,5},{5,6},{6,7},{7,8},{8,9},{9,10},{10,1... | collective-permute-start | bytes 49160 | tf_op jit(solution)/shard_map/ppermute | solution.py:14
  48.2 6.8 %collective-permute-start.12 = (f32[1,64,32]{1,2,0:T(8,128)S(1)}, f32[1,64,32]{1,2,0:T(8,128)S(1)}, u32[]{:S(2)}, u32[]{:S(2)}) collective-permute-start(f32[1,64,32]{1,2,0:T(8,128)S(1)} %fusion.58), channel_id=1, source_target_pairs={{0,3},{1,4},{2,5},{3,6},{4,7},{5,8},{6,9},{7,10},{8,11},{9,12},{10... | collective-permute-start | bytes 24584 | tf_op jit(solution)/shard_map/ppermute | solution.py:14
  62.4 6.6 %collective-permute-start.26 = (f32[35,2048]{1,0:T(8,128)S(1)}, f32[35,2048]{1,0:T(8,128)S(1)}, u32[]{:S(2)}, u32[]{:S(2)}) collective-permute-start(f32[35,2048]{1,0:T(8,128)S(1)} %get-tuple-element.164), channel_id=1, source_target_pairs={{0,1},{1,2},{2,3},{3,4},{4,5},{5,6},{6,7},{7,8},{8,9},{9,10},{10,1... | collective-permute-start | bytes 860168 | tf_op jit(solution)/shard_map/ppermute | solution.py:24
  69.2 3.3 %collective-permute-start.20 = (f32[1,64,32]{1,2,0:T(8,128)S(1)}, f32[1,64,32]{1,2,0:T(8,128)S(1)}, u32[]{:S(2)}, u32[]{:S(2)}) collective-permute-start(f32[1,64,32]{1,2,0:T(8,128)S(1)} %fusion.52), channel_id=1, source_target_pairs={{6,0},{7,1},{8,2},{9,3},{10,4},{11,5},{12,6},{13,7},{14,8},{15,9},... | collective-permute-start | bytes 24584 | tf_op jit(solution)/shard_map/ppermute | solution.py:14
  86.8 4.9 %collective-permute-done.24 = f32[1,64,32]{1,2,0:T(8,128)S(1)} collective-permute-done((f32[1,64,32]{1,2,0:T(8,128)S(1)}, f32[1,64,32]{1,2,0:T(8,128)S(1)}, u32[]{:S(2)}, u32[]{:S(2)}) %collective-permute-start.24) | collective-permute-done | bytes 8224 | tf_op jit(solution)/shard_map/ppermute | solution.py:14
  95.1 10.3 %collective-permute-start.17 = (f32[1,64,32]{1,2,0:T(8,128)S(1)}, f32[1,64,32]{1,2,0:T(8,128)S(1)}, u32[]{:S(2)}, u32[]{:S(2)}) collective-permute-start(f32[1,64,32]{1,2,0:T(8,128)S(1)} %fusion.52), channel_id=1, source_target_pairs={{0,6},{1,7},{2,8},{3,9},{4,10},{5,11},{6,12},{7,13},{8,14},{9,15},... | collective-permute-start | bytes 24584 | tf_op jit(solution)/shard_map/ppermute | solution.py:14
  106.2 7.3 %collective-permute-start.7 = (f32[3,64,32]{1,2,0:T(8,128)S(1)}, f32[3,64,32]{1,2,0:T(8,128)S(1)}, u32[]{:S(2)}, u32[]{:S(2)}) collective-permute-start(f32[3,64,32]{1,2,0:T(8,128)S(1)} %copy-done.11), channel_id=1, source_target_pairs={{1,0},{2,1},{3,2},{4,3},{5,4},{6,5},{7,6},{8,7},{9,8},{10,9},{11,1... | collective-permute-start | bytes 73736 | tf_op jit(solution)/shard_map/ppermute | solution.py:14
  113.9 4.9 %collective-permute-start.6 = (f32[3,64,32]{1,2,0:T(8,128)S(1)}, f32[3,64,32]{1,2,0:T(8,128)S(1)}, u32[]{:S(2)}, u32[]{:S(2)}) collective-permute-start(f32[3,64,32]{1,2,0:T(8,128)S(1)} %copy-done.10), channel_id=1, source_target_pairs={{0,1},{1,2},{2,3},{3,4},{4,5},{5,6},{6,7},{7,8},{8,9},{9,10},{10,1... | collective-permute-start | bytes 73736 | tf_op jit(solution)/shard_map/ppermute | solution.py:14
  122.7 4.5 %collective-permute-start.4 = (f32[3,64,32]{1,2,0:T(8,128)S(1)}, f32[3,64,32]{1,2,0:T(8,128)S(1)}, u32[]{:S(2)}, u32[]{:S(2)}) collective-permute-start(f32[3,64,32]{1,2,0:T(8,128)S(1)} %copy-done.8), channel_id=1, source_target_pairs={{0,1},{1,2},{2,3},{3,4},{4,5},{5,6},{6,7},{7,8},{8,9},{9,10},{10,1... | collective-permute-start | bytes 73736 | tf_op jit(solution)/shard_map/ppermute | solution.py:14
  130.6 4.5 %collective-permute-start.2 = (f32[3,64,32]{1,2,0:T(8,128)S(1)}, f32[3,64,32]{1,2,0:T(8,128)S(1)}, u32[]{:S(2)}, u32[]{:S(2)}) collective-permute-start(f32[3,64,32]{1,2,0:T(8,128)S(1)} %copy-done.6), channel_id=1, source_target_pairs={{0,1},{1,2},{2,3},{3,4},{4,5},{5,6},{6,7},{7,8},{8,9},{9,10},{10,1... | collective-permute-start | bytes 73736 | tf_op jit(solution)/shard_map/ppermute | solution.py:14
  138.8 4.7 %collective-permute-start = (f32[3,64,32]{1,2,0:T(8,128)S(1)}, f32[3,64,32]{1,2,0:T(8,128)S(1)}, u32[]{:S(2)}, u32[]{:S(2)}) collective-permute-start(f32[3,64,32]{1,2,0:T(8,128)S(1)} %copy-done.4), channel_id=1, source_target_pairs={{0,1},{1,2},{2,3},{3,4},{4,5},{5,6},{6,7},{7,8},{8,9},{9,10},{10,1... | collective-permute-start | bytes 73736 | tf_op jit(solution)/shard_map/ppermute | solution.py:14
  150.0 156.7 %while.13 = (s32[]{:T(128)}, f32[16,32,2,128]{3,1,2,0:T(8,128)S(1)}, s32[16]{0:T(128)S(1)}, s32[27,32]{0,1:T(8,128)}, bf16[32,64,128]{2,0,1:T(8,128)(2,1)S(1)}, ...) while((s32[]{:T(128)}, ...), condition=%wide.region_1.2_spmd.clone, body=%wide.region_0.1_spmd.clone.sunk | while | flops 68347216 | bytes 1971609 | solution.py:109
  156.9 2.9 fusion.283
  176.5 2.9 fusion.283
  186.2 2.9 fusion.283
  215.6 2.9 fusion.283
  225.4 2.9 fusion.283
  235.2 2.9 fusion.283
  254.8 2.9 fusion.283
  264.6 2.9 fusion.283
  274.4 2.9 fusion.283
  284.2 2.9 fusion.283
  294.0 2.9 fusion.283
  303.7 2.9 fusion.283
  (402 shorter events, 150.1 us)
Async XLA Ops:
  3.8 65.4 %collective-permute-start.11 = (f32[2,64,32]{1,2,0:T(8,128)S(1)}, f32[2,64,32]{1,2,0:T(8,128)}, u32[]{:S(2)}, u32[]{:S(2)}) collective-permute-start(f32[2,64,32]{1,2,0:T(8,128)S(1)} %fusion.41), channel_id=1, source_target_pairs={{2,0},{3,1},{4,2},{5,3},{6,4},{7,5},{8,6},{9,7},{10,8},{11,9},{12,... | collective-permute-start | bytes 49160 | tf_op jit(solution)/shard_map/ppermute | solution.py:14
  5.9 50.9 %collective-permute-start.10 = (f32[2,64,32]{1,2,0:T(8,128)S(1)}, f32[2,64,32]{1,2,0:T(8,128)S(1)}, u32[]{:S(2)}, u32[]{:S(2)}) collective-permute-start(f32[2,64,32]{1,2,0:T(8,128)S(1)} %fusion.41), channel_id=1, source_target_pairs={{1,0},{2,1},{3,2},{4,3},{5,4},{6,5},{7,6},{8,7},{9,8},{10,9},{11,1... | collective-permute-start | bytes 49160 | tf_op jit(solution)/shard_map/ppermute | solution.py:14
  8.8 50.9 %collective-permute-start.9 = (f32[2,64,32]{1,2,0:T(8,128)S(1)}, f32[2,64,32]{1,2,0:T(8,128)}, u32[]{:S(2)}, u32[]{:S(2)}) collective-permute-start(f32[2,64,32]{1,2,0:T(8,128)S(1)} %fusion.41), channel_id=1, source_target_pairs={{0,1},{1,2},{2,3},{3,4},{4,5},{5,6},{6,7},{7,8},{8,9},{9,10},{10,1... | collective-permute-start | bytes 49160 | tf_op jit(solution)/shard_map/ppermute | solution.py:14
  12.7 106.6 %collective-permute-start.8 = (f32[2,64,32]{1,2,0:T(8,128)S(1)}, f32[2,64,32]{1,2,0:T(8,128)}, u32[]{:S(2)}, u32[]{:S(2)}) collective-permute-start(f32[2,64,32]{1,2,0:T(8,128)S(1)} %fusion.41), channel_id=1, source_target_pairs={{0,2},{1,3},{2,4},{3,5},{4,6},{5,7},{6,8},{7,9},{8,10},{9,11},{10,... | collective-permute-start | bytes 49160 | tf_op jit(solution)/shard_map/ppermute | solution.py:14
  15.8 17.4 %collective-permute-start.16 = (f32[1,64,32]{1,2,0:T(8,128)S(1)}, f32[1,64,32]{1,2,0:T(8,128)}, u32[]{:S(2)}, u32[]{:S(2)}) collective-permute-start(f32[1,64,32]{1,2,0:T(8,128)S(1)} %fusion.58), channel_id=1, source_target_pairs={{0,1},{1,0},{2,3},{3,2},{4,5},{5,4},{6,7},{7,6},{8,9},{9,8},{10,11... | collective-permute-start | bytes 24584 | tf_op jit(solution)/shard_map/ppermute | solution.py:33
  33.3 5.1 %collective-permute-start.15 = (f32[1,64,32]{1,2,0:T(8,128)S(1)}, f32[1,64,32]{1,2,0:T(8,128)S(1)}, u32[]{:S(2)}, u32[]{:S(2)}) collective-permute-start(f32[1,64,32]{1,2,0:T(8,128)S(1)} %fusion.58), channel_id=1, source_target_pairs={{3,0},{4,1},{5,2},{6,3},{7,4},{8,5},{9,6},{10,7},{11,8},{12,9},{13... | collective-permute-start | bytes 24584 | tf_op jit(solution)/shard_map/ppermute | solution.py:14
  38.4 5.4 %collective-permute-start.14 = (f32[1,64,32]{1,2,0:T(8,128)S(1)}, f32[1,64,32]{1,2,0:T(8,128)S(1)}, u32[]{:S(2)}, u32[]{:S(2)}) collective-permute-start(f32[1,64,32]{1,2,0:T(8,128)S(1)} %fusion.58), channel_id=1, source_target_pairs={{2,0},{3,1},{4,2},{5,3},{6,4},{7,5},{8,6},{9,7},{10,8},{11,9},{12,... | collective-permute-start | bytes 24584 | tf_op jit(solution)/shard_map/ppermute | solution.py:14
  43.7 4.5 %collective-permute-start.13 = (f32[1,64,32]{1,2,0:T(8,128)S(1)}, f32[1,64,32]{1,2,0:T(8,128)S(1)}, u32[]{:S(2)}, u32[]{:S(2)}) collective-permute-start(f32[1,64,32]{1,2,0:T(8,128)S(1)} %fusion.58), channel_id=1, source_target_pairs={{0,2},{1,3},{2,4},{3,5},{4,6},{5,7},{6,8},{7,9},{8,10},{9,11},{10,... | collective-permute-start | bytes 24584 | tf_op jit(solution)/shard_map/ppermute | solution.py:14
  48.2 65.7 %collective-permute-start.12 = (f32[1,64,32]{1,2,0:T(8,128)S(1)}, f32[1,64,32]{1,2,0:T(8,128)S(1)}, u32[]{:S(2)}, u32[]{:S(2)}) collective-permute-start(f32[1,64,32]{1,2,0:T(8,128)S(1)} %fusion.58), channel_id=1, source_target_pairs={{0,3},{1,4},{2,5},{3,6},{4,7},{5,8},{6,9},{7,10},{8,11},{9,12},{10... | collective-permute-start | bytes 24584 | tf_op jit(solution)/shard_map/ppermute | solution.py:14
  56.9 92.4 %collective-permute-start.27 = (f32[35,2048]{1,0:T(8,128)}, f32[35,2048]{1,0:T(8,128)S(1)}, u32[]{:S(2)}, u32[]{:S(2)}) collective-permute-start(f32[35,2048]{1,0:T(8,128)} %get-tuple-element.165), channel_id=1, source_target_pairs={{1,0},{2,1},{3,2},{4,3},{5,4},{6,5},{7,6},{8,7},{9,8},{10,9},{11,1... | collective-permute-start | bytes 860168 | tf_op jit(solution)/shard_map/ppermute | solution.py:25
  62.4 86.8 %collective-permute-start.26 = (f32[35,2048]{1,0:T(8,128)S(1)}, f32[35,2048]{1,0:T(8,128)S(1)}, u32[]{:S(2)}, u32[]{:S(2)}) collective-permute-start(f32[35,2048]{1,0:T(8,128)S(1)} %get-tuple-element.164), channel_id=1, source_target_pairs={{0,1},{1,2},{2,3},{3,4},{4,5},{5,6},{6,7},{7,8},{8,9},{9,10},{10,1... | collective-permute-start | bytes 860168 | tf_op jit(solution)/shard_map/ppermute | solution.py:24
  69.2 6.3 %collective-permute-start.20 = (f32[1,64,32]{1,2,0:T(8,128)S(1)}, f32[1,64,32]{1,2,0:T(8,128)S(1)}, u32[]{:S(2)}, u32[]{:S(2)}) collective-permute-start(f32[1,64,32]{1,2,0:T(8,128)S(1)} %fusion.52), channel_id=1, source_target_pairs={{6,0},{7,1},{8,2},{9,3},{10,4},{11,5},{12,6},{13,7},{14,8},{15,9},... | collective-permute-start | bytes 24584 | tf_op jit(solution)/shard_map/ppermute | solution.py:14
  75.5 4.5 %collective-permute-start.19 = (f32[1,64,32]{1,2,0:T(8,128)S(1)}, f32[1,64,32]{1,2,0:T(8,128)S(1)}, u32[]{:S(2)}, u32[]{:S(2)}) collective-permute-start(f32[1,64,32]{1,2,0:T(8,128)S(1)} %fusion.52), channel_id=1, source_target_pairs={{4,0},{5,1},{6,2},{7,3},{8,4},{9,5},{10,6},{11,7},{12,8},{13,9},{1... | collective-permute-start | bytes 24584 | tf_op jit(solution)/shard_map/ppermute | solution.py:14
  80.0 4.5 %collective-permute-start.18 = (f32[1,64,32]{1,2,0:T(8,128)S(1)}, f32[1,64,32]{1,2,0:T(8,128)S(1)}, u32[]{:S(2)}, u32[]{:S(2)}) collective-permute-start(f32[1,64,32]{1,2,0:T(8,128)S(1)} %fusion.52), channel_id=1, source_target_pairs={{0,4},{1,5},{2,6},{3,7},{4,8},{5,9},{6,10},{7,11},{8,12},{9,13},{1... | collective-permute-start | bytes 24584 | tf_op jit(solution)/shard_map/ppermute | solution.py:14
  85.3 6.4 %collective-permute-start.24 = (f32[1,64,32]{1,2,0:T(8,128)S(1)}, f32[1,64,32]{1,2,0:T(8,128)S(1)}, u32[]{:S(2)}, u32[]{:S(2)}) collective-permute-start(f32[1,64,32]{1,2,0:T(8,128)S(1)} %fusion.46), channel_id=1, source_target_pairs={{8,0},{9,1},{10,2},{11,3},{12,4},{13,5},{14,6},{15,7},{24,16},{25,... | collective-permute-start | bytes 24584 | tf_op jit(solution)/shard_map/ppermute | solution.py:14
  95.1 11.2 %collective-permute-start.17 = (f32[1,64,32]{1,2,0:T(8,128)S(1)}, f32[1,64,32]{1,2,0:T(8,128)S(1)}, u32[]{:S(2)}, u32[]{:S(2)}) collective-permute-start(f32[1,64,32]{1,2,0:T(8,128)S(1)} %fusion.52), channel_id=1, source_target_pairs={{0,6},{1,7},{2,8},{3,9},{4,10},{5,11},{6,12},{7,13},{8,14},{9,15},... | collective-permute-start | bytes 24584 | tf_op jit(solution)/shard_map/ppermute | solution.py:14
  106.2 16.5 %collective-permute-start.7 = (f32[3,64,32]{1,2,0:T(8,128)S(1)}, f32[3,64,32]{1,2,0:T(8,128)S(1)}, u32[]{:S(2)}, u32[]{:S(2)}) collective-permute-start(f32[3,64,32]{1,2,0:T(8,128)S(1)} %copy-done.11), channel_id=1, source_target_pairs={{1,0},{2,1},{3,2},{4,3},{5,4},{6,5},{7,6},{8,7},{9,8},{10,9},{11,1... | collective-permute-start | bytes 73736 | tf_op jit(solution)/shard_map/ppermute | solution.py:14
  113.9 13.8 %collective-permute-start.6 = (f32[3,64,32]{1,2,0:T(8,128)S(1)}, f32[3,64,32]{1,2,0:T(8,128)S(1)}, u32[]{:S(2)}, u32[]{:S(2)}) collective-permute-start(f32[3,64,32]{1,2,0:T(8,128)S(1)} %copy-done.10), channel_id=1, source_target_pairs={{0,1},{1,2},{2,3},{3,4},{4,5},{5,6},{6,7},{7,8},{8,9},{9,10},{10,1... | collective-permute-start | bytes 73736 | tf_op jit(solution)/shard_map/ppermute | solution.py:14
  119.3 11.2 %collective-permute-start.5 = (f32[3,64,32]{1,2,0:T(8,128)S(1)}, f32[3,64,32]{1,2,0:T(8,128)S(1)}, u32[]{:S(2)}, u32[]{:S(2)}) collective-permute-start(f32[3,64,32]{1,2,0:T(8,128)S(1)} %copy-done.9), channel_id=1, source_target_pairs={{1,0},{2,1},{3,2},{4,3},{5,4},{6,5},{7,6},{8,7},{9,8},{10,9},{11,1... | collective-permute-start | bytes 73736 | tf_op jit(solution)/shard_map/ppermute | solution.py:14
  122.7 13.1 %collective-permute-start.4 = (f32[3,64,32]{1,2,0:T(8,128)S(1)}, f32[3,64,32]{1,2,0:T(8,128)S(1)}, u32[]{:S(2)}, u32[]{:S(2)}) collective-permute-start(f32[3,64,32]{1,2,0:T(8,128)S(1)} %copy-done.8), channel_id=1, source_target_pairs={{0,1},{1,2},{2,3},{3,4},{4,5},{5,6},{6,7},{7,8},{8,9},{9,10},{10,1... | collective-permute-start | bytes 73736 | tf_op jit(solution)/shard_map/ppermute | solution.py:14
  127.7 11.1 %collective-permute-start.3 = (f32[3,64,32]{1,2,0:T(8,128)S(1)}, f32[3,64,32]{1,2,0:T(8,128)S(1)}, u32[]{:S(2)}, u32[]{:S(2)}) collective-permute-start(f32[3,64,32]{1,2,0:T(8,128)S(1)} %copy-done.7), channel_id=1, source_target_pairs={{1,0},{2,1},{3,2},{4,3},{5,4},{6,5},{7,6},{8,7},{9,8},{10,9},{11,1... | collective-permute-start | bytes 73736 | tf_op jit(solution)/shard_map/ppermute | solution.py:14
  130.6 13.8 %collective-permute-start.2 = (f32[3,64,32]{1,2,0:T(8,128)S(1)}, f32[3,64,32]{1,2,0:T(8,128)S(1)}, u32[]{:S(2)}, u32[]{:S(2)}) collective-permute-start(f32[3,64,32]{1,2,0:T(8,128)S(1)} %copy-done.6), channel_id=1, source_target_pairs={{0,1},{1,2},{2,3},{3,4},{4,5},{5,6},{6,7},{7,8},{8,9},{9,10},{10,1... | collective-permute-start | bytes 73736 | tf_op jit(solution)/shard_map/ppermute | solution.py:14
  135.8 10.2 %collective-permute-start.1 = (f32[3,64,32]{1,2,0:T(8,128)S(1)}, f32[3,64,32]{1,2,0:T(8,128)S(1)}, u32[]{:S(2)}, u32[]{:S(2)}) collective-permute-start(f32[3,64,32]{1,2,0:T(8,128)S(1)} %copy-done.5), channel_id=1, source_target_pairs={{1,0},{2,1},{3,2},{4,3},{5,4},{6,5},{7,6},{8,7},{9,8},{10,9},{11,1... | collective-permute-start | bytes 73736 | tf_op jit(solution)/shard_map/ppermute | solution.py:14
  138.8 8.4 %collective-permute-start = (f32[3,64,32]{1,2,0:T(8,128)S(1)}, f32[3,64,32]{1,2,0:T(8,128)S(1)}, u32[]{:S(2)}, u32[]{:S(2)}) collective-permute-start(f32[3,64,32]{1,2,0:T(8,128)S(1)} %copy-done.4), channel_id=1, source_target_pairs={{0,1},{1,2},{2,3},{3,4},{4,5},{5,6},{6,7},{7,8},{8,9},{9,10},{10,1... | collective-permute-start | bytes 73736 | tf_op jit(solution)/shard_map/ppermute | solution.py:14
  (36 other events, 828.2 us)
where the time goes:
time: 312 us; the launch traced here: 308 us
  starting transfers between devices  89 us (29%)
  matrix products  68.9 us (22%)
  loops' own time  52.5 us (17%)
  local copies, waits for them, and re-layouts  41.8 us (13%)
  other arithmetic  30 us (10%)
  waiting for transfers between devices  17.4 us (6%)
  between operations  8.8 us (3%)
    ppermute x24, starting transfers between devices, shifted(): return lax.ppermute(x, axis, pairs)  80.3 us
    another operation x1, loops' own time, local(): near_parts = lax.map(near_group, starts)  52.5 us
    dot_general x16, matrix products, near_group(): jnp.einsum('gspq,rgsq->rgp', block, chosen, preferred_element_type=jnp.fl...  46.8 us
    ppermute x24, waiting for transfers between devices, shifted(): return lax.ppermute(x, axis, pairs)  15.7 us
    dot_general x32, matrix products, couple(): term = jnp.einsum('kj,njr->nkr', table[which], piece, precision=highest)  15.3 us
    select_n x16, other arithmetic, near_group(): chosen = sources[:, picks] * used[None, :, :, None]  12.4 us
    gather x32, local copies, waits for them, and re-layouts, near_group(): spots = places[:, picks]  10.4 us
    add x16, other arithmetic, near_group(): picks = (leaf_ids[None, :] + reach + offsets).T  10.4 us
  transfers between devices with their start and end apart: 28, of which 10 were waited for; matrix products, arithmetic and copies ran while one was open for 10% of the time, Pallas kernels for 0%

commit v1 on v0

--- a/solution.py
+++ b/solution.py
@@ -1,6 +1,10 @@
+import functools
+
 import jax
 import jax.numpy as jnp
 from jax import lax
+from jax.experimental import pallas as pl
+from jax.experimental.pallas import tpu as pltpu
 from jax.sharding import PartitionSpec as P
 
 decay_rate = 1.7320508075688772 / 0.15
@@ -33,12 +37,122 @@
     return lax.ppermute(value, axis, pairs)
 
 
-def matern(targets, spots):
-    gap_x = targets[0] - spots[0]
-    gap_y = targets[1] - spots[1]
-    gap_z = targets[2] - spots[2]
-    scaled = decay_rate * jnp.sqrt(gap_x * gap_x + gap_y * gap_y + gap_z * gap_z)
-    return ((1.0 + scaled) * jnp.exp(-scaled)).astype(jnp.bfloat16)
+def split3(x):
+    one = x.astype(jnp.bfloat16).astype(jnp.float32)
+    two = (x - one).astype(jnp.bfloat16).astype(jnp.float32)
+    three = (x - one - two).astype(jnp.bfloat16).astype(jnp.float32)
+    return one, two, three
+
+
+def features(coords):
+    place = (coords - 0.5) * (decay_rate * 1.4426950408889634)
+    c1, c2, c3 = split3(place)
+    square = place * place
+    n1, n2, n3 = split3(square[0:1] + square[1:2] + square[2:3])
+    ones = jnp.ones_like(n1)
+    pad = jnp.zeros((8, coords.shape[1]), jnp.float32)
+    source = jnp.concatenate([c1, c1, c2, c2, c1, c3, n1, n2, n3, ones, ones, ones, pad], axis=0)
+    target = jnp.concatenate(
+        [-2 * c1, -2 * c2, -2 * c1, -2 * c2, -2 * c3, -2 * c1, ones, ones, ones, n1, n2, n3, pad],
+        axis=0,
+    )
+    return source, target
+
+
+def near_kernel(
+    chunk,
+    offsets_ref,
+    count_ref,
+    charges_ref,
+    before_ref,
+    after_ref,
+    coords_ref,
+    coords_before_ref,
+    coords_after_ref,
+    basis_ref,
+    coef_ref,
+    out_ref,
+    src_ref,
+    tgt_ref,
+    chg_ref,
+):
+    leaves = coef_ref.shape[0]
+    width = charges_ref.shape[1]
+    size = width // leaves
+    reach = leaves // 2
+    slots = offsets_ref.shape[0]
+    start = 0
+    for piece, place in (
+        (before_ref, coords_before_ref),
+        (charges_ref, coords_ref),
+        (after_ref, coords_after_ref),
+    ):
+        source, target = features(place[...])
+        for n in range(piece.shape[1] // size):
+            cut = slice(n * size, (n + 1) * size)
+            chg_ref[start + n] = piece[:, cut].astype(jnp.bfloat16)
+            src_ref[start + n] = source[:, cut].T.astype(jnp.bfloat16)
+            if piece is charges_ref:
+                tgt_ref[n] = target[:, cut].astype(jnp.bfloat16)
+        start += piece.shape[1] // size
+    chg_ref[start] = jnp.zeros(chg_ref.shape[1:], jnp.bfloat16)
+
+    def leaf_step(i, _):
+        count = count_ref[i]
+        target = tgt_ref[i]
+
+        def chunk_step(k, total):
+            picks = []
+            used = []
+            for s in range(chunk):
+                slot = k * chunk + s
+                pick = jnp.where(
+                    slot < count, i + reach + offsets_ref[jnp.minimum(slot, slots - 1), i], start
+                )
+                picks.append(pick)
+                used.append(jnp.minimum(pick, start - 1))
+            for s in range(chunk):
+                dist = jnp.dot(src_ref[used[s]], target, preferred_element_type=jnp.float32)
+                dist = jnp.maximum(dist, 1e-12)
+                gap = dist * lax.rsqrt(dist)
+                block = ((1.0 + gap * 0.6931471805599453) * jnp.exp2(-gap)).astype(jnp.bfloat16)
+                total = total + jnp.dot(
+                    chg_ref[picks[s]], block, preferred_element_type=jnp.float32
+                )
+            return total
+
+        cut = pl.ds(pl.multiple_of(i * size, size), size)
+        total = jnp.dot(
+            coef_ref[i].astype(jnp.bfloat16), basis_ref[:, cut], preferred_element_type=jnp.float32
+        )
+        total = lax.fori_loop(0, (count + chunk - 1) // chunk, chunk_step, total)
+        out_ref[:, cut] = total
+        return 0
+
+    lax.fori_loop(0, leaves, leaf_step, 0)
+
+
+def near_field(charges, before, after, coords, coords_before, coords_after, near_offsets,
+               near_count, basis, coef, chunk=5):
+    leaves = near_count.shape[0]
+    columns, width = charges.shape
+    size = width // leaves
+    vmem = pl.BlockSpec(memory_space=pltpu.VMEM)
+    smem = pl.BlockSpec(memory_space=pltpu.SMEM)
+    return pl.pallas_call(
+        functools.partial(near_kernel, chunk),
+        out_shape=jax.ShapeDtypeStruct((columns, width), jnp.float32),
+        in_specs=[smem, smem] + [vmem] * 8,
+        out_specs=vmem,
+        scratch_shapes=[
+            pltpu.VMEM((2 * leaves, size, 32), jnp.bfloat16),
+            pltpu.VMEM((leaves, 32, size), jnp.bfloat16),
+            pltpu.VMEM((2 * leaves + 1, columns, size), jnp.bfloat16),
+        ],
+        compiler_params=pltpu.CompilerParams(vmem_limit_bytes=40 * 2**20),
+        name="near",
+    )(near_offsets, near_count, charges, before, after, coords, coords_before, coords_after,
+      basis, coef)
 
 
 def lift(lower, transfer, height):
@@ -87,27 +201,7 @@
     reach = leaf_count // 2
     packed = jnp.concatenate([charges, coords], axis=0)
     widened = with_halo(packed, ((("leaf", "sub"), 1),), reach * leaf_size)
-    spanned = leaf_count + 2 * reach
-    sources = widened[:columns].astype(jnp.bfloat16).reshape(columns, spanned, leaf_size)
-    places = widened[columns:].reshape(3, spanned, leaf_size)
-    group = max(1, leaf_count // 16)
-    starts = jnp.arange(0, leaf_count, group, dtype=jnp.int32)
-    slots = jnp.arange(near_offsets.shape[0], dtype=jnp.int32)
-
-    def near_group(start):
-        leaf_ids = start + jnp.arange(group, dtype=jnp.int32)
-        offsets = lax.dynamic_slice_in_dim(near_offsets, start, group, 1)
-        counts = lax.dynamic_slice_in_dim(near_count, start, group, 0)
-        picks = (leaf_ids[None, :] + reach + offsets).T
-        used = (slots[None, :] < counts[:, None]).astype(jnp.bfloat16)
-        chosen = sources[:, picks] * used[None, :, :, None]
-        spots = places[:, picks]
-        targets = lax.dynamic_slice_in_dim(places, start + reach, group, 1)
-        block = matern(targets[:, :, None, :, None], spots[:, :, :, None, :])
-        return jnp.einsum("gspq,rgsq->rgp", block, chosen, preferred_element_type=jnp.float32)
-
-    near_parts = lax.map(near_group, starts)
-    near_part = near_parts.transpose(1, 0, 2, 3).reshape(columns, width)
+    edge = reach * leaf_size
     charges_low = charges.astype(jnp.bfloat16).reshape(columns, leaf_count, leaf_size)
     basis_leaf = basis.reshape(basis.shape[0], leaf_count, leaf_size)
     levels = [
@@ -148,11 +242,18 @@
             first = jnp.einsum("jk,nkr->njr", transfer[height, 0], totals, precision=highest)
             second = jnp.einsum("jk,nkr->njr", transfer[height, 1], totals, precision=highest)
             totals = own + jnp.stack([first, second], 1).reshape(own.shape)
-    leaf_coef = totals.astype(jnp.bfloat16)
-    far_part = jnp.einsum(
-        "kns,nkr->rns", basis_leaf, leaf_coef, preferred_element_type=jnp.float32
-    ).reshape(columns, width)
-    return far_part + near_part
+    return near_field(
+        charges,
+        widened[:columns, :edge],
+        widened[:columns, edge + width :],
+        coords,
+        widened[columns:, :edge],
+        widened[columns:, edge + width :],
+        near_offsets,
+        near_count,
+        basis,
+        totals.transpose(0, 2, 1),
+    )
 
 
 def solution(mesh):

time: 312 us -> 218 us (0.70)
  the two profiles are of different devices: /device:TPU:11 before, /device:TPU:23 now
where the time goes in v1:
time: 218 us; the launch traced here: 214 us
  starting transfers between devices  87.2 us (40%)
  Pallas kernels  55.6 us (26%)
  waiting for transfers between devices  20.3 us (9%)
  matrix products  19.5 us (9%)
  local copies, waits for them, and re-layouts  18.3 us (8%)
  between operations  8.55 us (4%)
  other arithmetic  4.4 us (2%)
    ppermute x24, starting transfers between devices, shifted(): return lax.ppermute(x, axis, pairs)  79.8 us
    pallas_call x1, Pallas kernels, near_field(): pl.pallas_call(functools.partial(near_kernel, chunk), out_shape=jax.Shape...  55.6 us
    ppermute x24, waiting for transfers between devices, shifted(): return lax.ppermute(x, axis, pairs)  17.2 us
    dot_general x32, matrix products, couple(): term = jnp.einsum('kj,njr->nkr', table[which], piece, precision=highest)  13.7 us
    unnamed x66, local copies, waits for them, and re-layouts  13.2 us
    ppermute x1, starting transfers between devices, with_halo(): before = lax.ppermute(last, axis, up)  4.55 us
  transfers between devices with their start and end apart: 28, of which 9 were waited for; matrix products, arithmetic and copies ran while one was open for 12% of the time, Pallas kernels for 0%

profile of v1, /device:TPU:23, one launch (start us, length us, event | category | flops | bytes accessed | tf_op | source)
XLA Modules:
  0.0 213.9 jit_solution(965095965854419138)
XLA Ops:
  4.4 2.2 %collective-permute-start.13 = (f32[2,64,32]{1,2,0:T(8,128)S(1)}, f32[2,64,32]{1,2,0:T(8,128)}, u32[]{:S(2)}, u32[]{:S(2)}) collective-permute-start(f32[2,64,32]{1,2,0:T(8,128)S(1)} %fusion.29), channel_id=1, source_target_pairs={{2,0},{3,1},{4,2},{5,3},{6,4},{7,5},{8,6},{9,7},{10,8},{11,9},{12,... | collective-permute-start | bytes 49160 | tf_op jit(solution)/shard_map/ppermute | solution.py:18
  6.5 2.9 %collective-permute-start.12 = (f32[2,64,32]{1,2,0:T(8,128)S(1)}, f32[2,64,32]{1,2,0:T(8,128)S(1)}, u32[]{:S(2)}, u32[]{:S(2)}) collective-permute-start(f32[2,64,32]{1,2,0:T(8,128)S(1)} %fusion.29), channel_id=1, source_target_pairs={{1,0},{2,1},{3,2},{4,3},{5,4},{6,5},{7,6},{8,7},{9,8},{10,9},{11,1... | collective-permute-start | bytes 49160 | tf_op jit(solution)/shard_map/ppermute | solution.py:18
  9.4 3.9 %collective-permute-start.11 = (f32[2,64,32]{1,2,0:T(8,128)S(1)}, f32[2,64,32]{1,2,0:T(8,128)S(1)}, u32[]{:S(2)}, u32[]{:S(2)}) collective-permute-start(f32[2,64,32]{1,2,0:T(8,128)S(1)} %fusion.29), channel_id=1, source_target_pairs={{0,1},{1,2},{2,3},{3,4},{4,5},{5,6},{6,7},{7,8},{8,9},{9,10},{10,1... | collective-permute-start | bytes 49160 | tf_op jit(solution)/shard_map/ppermute | solution.py:18
  13.3 2.9 %collective-permute-start.10 = (f32[2,64,32]{1,2,0:T(8,128)S(1)}, f32[2,64,32]{1,2,0:T(8,128)}, u32[]{:S(2)}, u32[]{:S(2)}) collective-permute-start(f32[2,64,32]{1,2,0:T(8,128)S(1)} %fusion.29), channel_id=1, source_target_pairs={{0,2},{1,3},{2,4},{3,5},{4,6},{5,7},{6,8},{7,9},{8,10},{9,11},{10,... | collective-permute-start | bytes 49160 | tf_op jit(solution)/shard_map/ppermute | solution.py:18
  32.2 2.8 %collective-permute-start.17 = (f32[1,64,32]{1,2,0:T(8,128)S(1)}, f32[1,64,32]{1,2,0:T(8,128)S(1)}, u32[]{:S(2)}, u32[]{:S(2)}) collective-permute-start(f32[1,64,32]{1,2,0:T(8,128)S(1)} %fusion.46), channel_id=1, source_target_pairs={{3,0},{4,1},{5,2},{6,3},{7,4},{8,5},{9,6},{10,7},{11,8},{12,9},{13... | collective-permute-start | bytes 24584 | tf_op jit(solution)/shard_map/ppermute | solution.py:18
  35.1 2.1 collective-permute-done.17
  37.2 2.5 %collective-permute-start.16 = (f32[1,64,32]{1,2,0:T(8,128)S(1)}, f32[1,64,32]{1,2,0:T(8,128)S(1)}, u32[]{:S(2)}, u32[]{:S(2)}) collective-permute-start(f32[1,64,32]{1,2,0:T(8,128)S(1)} %fusion.46), channel_id=1, source_target_pairs={{2,0},{3,1},{4,2},{5,3},{6,4},{7,5},{8,6},{9,7},{10,8},{11,9},{12,... | collective-permute-start | bytes 24584 | tf_op jit(solution)/shard_map/ppermute | solution.py:18
  47.1 3.5 %collective-permute-start.14 = (f32[1,64,32]{1,2,0:T(8,128)S(1)}, f32[1,64,32]{1,2,0:T(8,128)S(1)}, u32[]{:S(2)}, u32[]{:S(2)}) collective-permute-start(f32[1,64,32]{1,2,0:T(8,128)S(1)} %fusion.46), channel_id=1, source_target_pairs={{0,3},{1,4},{2,5},{3,6},{4,7},{5,8},{6,9},{7,10},{8,11},{9,12},{10... | collective-permute-start | bytes 24584 | tf_op jit(solution)/shard_map/ppermute | solution.py:18
  51.7 4.6 %collective-permute-start = (f32[35,2048]{1,0:T(8,128)}, f32[35,2048]{1,0:T(8,128)S(1)}, u32[]{:S(2)}, u32[]{:S(2)}) collective-permute-start(f32[35,2048]{1,0:T(8,128)} %get-tuple-element.6), channel_id=1, source_target_pairs={{0,1},{1,2},{2,3},{3,4},{4,5},{5,6},{6,7},{7,8},{8,9},{9,10},{10,1... | collective-permute-start | bytes 860168 | tf_op jit(solution)/shard_map/ppermute | solution.py:28
  59.0 3.1 %collective-permute-done.23 = f32[1,64,32]{1,2,0:T(8,128)S(1)} collective-permute-done((f32[1,64,32]{1,2,0:T(8,128)S(1)}, f32[1,64,32]{1,2,0:T(8,128)S(1)}, u32[]{:S(2)}, u32[]{:S(2)}) %collective-permute-start.23) | collective-permute-done | bytes 8224 | tf_op jit(solution)/shard_map/ppermute | solution.py:37
  64.3 3.5 %collective-permute-start.22 = (f32[1,64,32]{1,2,0:T(8,128)S(1)}, f32[1,64,32]{1,2,0:T(8,128)S(1)}, u32[]{:S(2)}, u32[]{:S(2)}) collective-permute-start(f32[1,64,32]{1,2,0:T(8,128)S(1)} %fusion.40), channel_id=1, source_target_pairs={{6,0},{7,1},{8,2},{9,3},{10,4},{11,5},{12,6},{13,7},{14,8},{15,9},... | collective-permute-start | bytes 24584 | tf_op jit(solution)/shard_map/ppermute | solution.py:18
  68.7 4.4 %collective-permute-start.21 = (f32[1,64,32]{1,2,0:T(8,128)S(1)}, f32[1,64,32]{1,2,0:T(8,128)S(1)}, u32[]{:S(2)}, u32[]{:S(2)}) collective-permute-start(f32[1,64,32]{1,2,0:T(8,128)S(1)} %fusion.40), channel_id=1, source_target_pairs={{4,0},{5,1},{6,2},{7,3},{8,4},{9,5},{10,6},{11,7},{12,8},{13,9},{1... | collective-permute-start | bytes 24584 | tf_op jit(solution)/shard_map/ppermute | solution.py:18
  76.2 2.5 %collective-permute-done.20 = f32[1,64,32]{1,2,0:T(8,128)S(1)} collective-permute-done((f32[1,64,32]{1,2,0:T(8,128)S(1)}, f32[1,64,32]{1,2,0:T(8,128)S(1)}, u32[]{:S(2)}, u32[]{:S(2)}) %collective-permute-start.20) | collective-permute-done | bytes 8224 | tf_op jit(solution)/shard_map/ppermute | solution.py:18
  79.5 8.2 %collective-permute-start.26 = (f32[1,64,32]{1,2,0:T(8,128)S(1)}, f32[1,64,32]{1,2,0:T(8,128)S(1)}, u32[]{:S(2)}, u32[]{:S(2)}) collective-permute-start(f32[1,64,32]{1,2,0:T(8,128)S(1)} %fusion.34), channel_id=1, source_target_pairs={{8,0},{9,1},{10,2},{11,3},{12,4},{13,5},{14,6},{15,7},{24,16},{25,... | collective-permute-start | bytes 24584 | tf_op jit(solution)/shard_map/ppermute | solution.py:18
  90.1 3.9 %collective-permute-done.25 = f32[1,64,32]{1,2,0:T(8,128)S(1)} collective-permute-done((f32[1,64,32]{1,2,0:T(8,128)S(1)}, f32[1,64,32]{1,2,0:T(8,128)S(1)}, u32[]{:S(2)}, u32[]{:S(2)}) %collective-permute-start.25) | collective-permute-done | bytes 8224 | tf_op jit(solution)/shard_map/ppermute | solution.py:18
  96.5 3.7 %collective-permute-done.19 = f32[1,64,32]{1,2,0:T(8,128)S(1)} collective-permute-done((f32[1,64,32]{1,2,0:T(8,128)S(1)}, f32[1,64,32]{1,2,0:T(8,128)S(1)}, u32[]{:S(2)}, u32[]{:S(2)}) %collective-permute-start.19) | collective-permute-done | bytes 8224 | tf_op jit(solution)/shard_map/ppermute | solution.py:18
  100.2 10.7 %collective-permute-start.9 = (f32[3,64,32]{1,2,0:T(8,128)S(1)}, f32[3,64,32]{1,2,0:T(8,128)S(1)}, u32[]{:S(2)}, u32[]{:S(2)}) collective-permute-start(f32[3,64,32]{1,2,0:T(8,128)S(1)} %copy-done.14), channel_id=1, source_target_pairs={{1,0},{2,1},{3,2},{4,3},{5,4},{6,5},{7,6},{8,7},{9,8},{10,9},{11,1... | collective-permute-start | bytes 73736 | tf_op jit(solution)/shard_map/ppermute | solution.py:18
  111.9 4.4 %collective-permute-start.8 = (f32[3,64,32]{1,2,0:T(8,128)S(1)}, f32[3,64,32]{1,2,0:T(8,128)S(1)}, u32[]{:S(2)}, u32[]{:S(2)}) collective-permute-start(f32[3,64,32]{1,2,0:T(8,128)S(1)} %copy-done.13), channel_id=1, source_target_pairs={{0,1},{1,2},{2,3},{3,4},{4,5},{5,6},{6,7},{7,8},{8,9},{9,10},{10,1... | collective-permute-start | bytes 73736 | tf_op jit(solution)/shard_map/ppermute | solution.py:18
  117.5 2.0 collective-permute-start.7
  121.7 4.7 %collective-permute-start.6 = (f32[3,64,32]{1,2,0:T(8,128)S(1)}, f32[3,64,32]{1,2,0:T(8,128)S(1)}, u32[]{:S(2)}, u32[]{:S(2)}) collective-permute-start(f32[3,64,32]{1,2,0:T(8,128)S(1)} %copy-done.11), channel_id=1, source_target_pairs={{0,1},{1,2},{2,3},{3,4},{4,5},{5,6},{6,7},{7,8},{8,9},{9,10},{10,1... | collective-permute-start | bytes 73736 | tf_op jit(solution)/shard_map/ppermute | solution.py:18
  128.0 2.0 collective-permute-start.5
  132.2 4.7 %collective-permute-start.4 = (f32[3,64,32]{1,2,0:T(8,128)S(1)}, f32[3,64,32]{1,2,0:T(8,128)S(1)}, u32[]{:S(2)}, u32[]{:S(2)}) collective-permute-start(f32[3,64,32]{1,2,0:T(8,128)S(1)} %copy-done.9), channel_id=1, source_target_pairs={{0,1},{1,2},{2,3},{3,4},{4,5},{5,6},{6,7},{7,8},{8,9},{9,10},{10,1... | collective-permute-start | bytes 73736 | tf_op jit(solution)/shard_map/ppermute | solution.py:18
  143.2 4.8 %collective-permute-start.2 = (f32[3,64,32]{1,2,0:T(8,128)S(1)}, f32[3,64,32]{1,2,0:T(8,128)S(1)}, u32[]{:S(2)}, u32[]{:S(2)}) collective-permute-start(f32[3,64,32]{1,2,0:T(8,128)S(1)} %copy-done.7), channel_id=1, source_target_pairs={{0,1},{1,2},{2,3},{3,4},{4,5},{5,6},{6,7},{7,8},{8,9},{9,10},{10,1... | collective-permute-start | bytes 73736 | tf_op jit(solution)/shard_map/ppermute | solution.py:18
  158.3 55.6 %near.1 = f32[32,4096]{1,0:T(8,128)} custom-call(s32[27,32]{1,0:T(8,128)S(1)} %copy-done.3, s32[32]{0:T(128)S(1)} %copy-done.4, f32[32,4096]{1,0:T(8,128)S(1)} %copy-done, f32[32,2048]{1,0:T(8,128)S(1)} %slice.591.before_ref, f32[32,2048]{1,0:T(8,128)S(1)} %slice.593.after_ref, f32[3,4096]{1,0:T(4,128)S(1)} %copy-done.2, ...), custom_call_target="tpu_custom_call" | custom-call | tf_op jit(solution)/shard_map/near/pallas_call | solution.py:142
  (190 shorter events, 59.8 us)
Async XLA Ops:
  4.4 59.9 %collective-permute-start.13 = (f32[2,64,32]{1,2,0:T(8,128)S(1)}, f32[2,64,32]{1,2,0:T(8,128)}, u32[]{:S(2)}, u32[]{:S(2)}) collective-permute-start(f32[2,64,32]{1,2,0:T(8,128)S(1)} %fusion.29), channel_id=1, source_target_pairs={{2,0},{3,1},{4,2},{5,3},{6,4},{7,5},{8,6},{9,7},{10,8},{11,9},{12,... | collective-permute-start | bytes 49160 | tf_op jit(solution)/shard_map/ppermute | solution.py:18
  6.5 45.1 %collective-permute-start.12 = (f32[2,64,32]{1,2,0:T(8,128)S(1)}, f32[2,64,32]{1,2,0:T(8,128)S(1)}, u32[]{:S(2)}, u32[]{:S(2)}) collective-permute-start(f32[2,64,32]{1,2,0:T(8,128)S(1)} %fusion.29), channel_id=1, source_target_pairs={{1,0},{2,1},{3,2},{4,3},{5,4},{6,5},{7,6},{8,7},{9,8},{10,9},{11,1... | collective-permute-start | bytes 49160 | tf_op jit(solution)/shard_map/ppermute | solution.py:18
  9.4 47.8 %collective-permute-start.11 = (f32[2,64,32]{1,2,0:T(8,128)S(1)}, f32[2,64,32]{1,2,0:T(8,128)S(1)}, u32[]{:S(2)}, u32[]{:S(2)}) collective-permute-start(f32[2,64,32]{1,2,0:T(8,128)S(1)} %fusion.29), channel_id=1, source_target_pairs={{0,1},{1,2},{2,3},{3,4},{4,5},{5,6},{6,7},{7,8},{8,9},{9,10},{10,1... | collective-permute-start | bytes 49160 | tf_op jit(solution)/shard_map/ppermute | solution.py:18
  13.3 103.6 %collective-permute-start.10 = (f32[2,64,32]{1,2,0:T(8,128)S(1)}, f32[2,64,32]{1,2,0:T(8,128)}, u32[]{:S(2)}, u32[]{:S(2)}) collective-permute-start(f32[2,64,32]{1,2,0:T(8,128)S(1)} %fusion.29), channel_id=1, source_target_pairs={{0,2},{1,3},{2,4},{3,5},{4,6},{5,7},{6,8},{7,9},{8,10},{9,11},{10,... | collective-permute-start | bytes 49160 | tf_op jit(solution)/shard_map/ppermute | solution.py:18
  16.5 15.7 %collective-permute-start.18 = (f32[1,64,32]{1,2,0:T(8,128)S(1)}, f32[1,64,32]{1,2,0:T(8,128)S(1)}, u32[]{:S(2)}, u32[]{:S(2)}) collective-permute-start(f32[1,64,32]{1,2,0:T(8,128)S(1)} %fusion.46), channel_id=1, source_target_pairs={{0,1},{1,0},{2,3},{3,2},{4,5},{5,4},{6,7},{7,6},{8,9},{9,8},{10,11... | collective-permute-start | bytes 24584 | tf_op jit(solution)/shard_map/ppermute | solution.py:37
  32.2 5.1 %collective-permute-start.17 = (f32[1,64,32]{1,2,0:T(8,128)S(1)}, f32[1,64,32]{1,2,0:T(8,128)S(1)}, u32[]{:S(2)}, u32[]{:S(2)}) collective-permute-start(f32[1,64,32]{1,2,0:T(8,128)S(1)} %fusion.46), channel_id=1, source_target_pairs={{3,0},{4,1},{5,2},{6,3},{7,4},{8,5},{9,6},{10,7},{11,8},{12,9},{13... | collective-permute-start | bytes 24584 | tf_op jit(solution)/shard_map/ppermute | solution.py:18
  37.2 5.4 %collective-permute-start.16 = (f32[1,64,32]{1,2,0:T(8,128)S(1)}, f32[1,64,32]{1,2,0:T(8,128)S(1)}, u32[]{:S(2)}, u32[]{:S(2)}) collective-permute-start(f32[1,64,32]{1,2,0:T(8,128)S(1)} %fusion.46), channel_id=1, source_target_pairs={{2,0},{3,1},{4,2},{5,3},{6,4},{7,5},{8,6},{9,7},{10,8},{11,9},{12,... | collective-permute-start | bytes 24584 | tf_op jit(solution)/shard_map/ppermute | solution.py:18
  47.1 64.2 %collective-permute-start.14 = (f32[1,64,32]{1,2,0:T(8,128)S(1)}, f32[1,64,32]{1,2,0:T(8,128)S(1)}, u32[]{:S(2)}, u32[]{:S(2)}) collective-permute-start(f32[1,64,32]{1,2,0:T(8,128)S(1)} %fusion.46), channel_id=1, source_target_pairs={{0,3},{1,4},{2,5},{3,6},{4,7},{5,8},{6,9},{7,10},{8,11},{9,12},{10... | collective-permute-start | bytes 24584 | tf_op jit(solution)/shard_map/ppermute | solution.py:18
  51.7 105.6 %collective-permute-start = (f32[35,2048]{1,0:T(8,128)}, f32[35,2048]{1,0:T(8,128)S(1)}, u32[]{:S(2)}, u32[]{:S(2)}) collective-permute-start(f32[35,2048]{1,0:T(8,128)} %get-tuple-element.6), channel_id=1, source_target_pairs={{0,1},{1,2},{2,3},{3,4},{4,5},{5,6},{6,7},{7,8},{8,9},{9,10},{10,1... | collective-permute-start | bytes 860168 | tf_op jit(solution)/shard_map/ppermute | solution.py:28
  57.2 5.0 %collective-permute-start.23 = (f32[1,64,32]{1,2,0:T(8,128)S(1)}, f32[1,64,32]{1,2,0:T(8,128)S(1)}, u32[]{:S(2)}, u32[]{:S(2)}) collective-permute-start(f32[1,64,32]{1,2,0:T(8,128)S(1)} %fusion.40), channel_id=1, source_target_pairs={{0,2},{1,3},{2,0},{3,1},{4,6},{5,7},{6,4},{7,5},{8,10},{9,11},{10,... | collective-permute-start | bytes 24584 | tf_op jit(solution)/shard_map/ppermute | solution.py:37
  62.2 95.1 %collective-permute-start.1 = (f32[35,2048]{1,0:T(8,128)S(1)}, f32[35,2048]{1,0:T(8,128)S(1)}, u32[]{:S(2)}, u32[]{:S(2)}) collective-permute-start(f32[35,2048]{1,0:T(8,128)S(1)} %get-tuple-element.5), channel_id=1, source_target_pairs={{1,0},{2,1},{3,2},{4,3},{5,4},{6,5},{7,6},{8,7},{9,8},{10,9},{11,1... | collective-permute-start | bytes 860168 | tf_op jit(solution)/shard_map/ppermute | solution.py:29
  68.7 5.2 %collective-permute-start.21 = (f32[1,64,32]{1,2,0:T(8,128)S(1)}, f32[1,64,32]{1,2,0:T(8,128)S(1)}, u32[]{:S(2)}, u32[]{:S(2)}) collective-permute-start(f32[1,64,32]{1,2,0:T(8,128)S(1)} %fusion.40), channel_id=1, source_target_pairs={{4,0},{5,1},{6,2},{7,3},{8,4},{9,5},{10,6},{11,7},{12,8},{13,9},{1... | collective-permute-start | bytes 24584 | tf_op jit(solution)/shard_map/ppermute | solution.py:18
  73.9 4.7 %collective-permute-start.20 = (f32[1,64,32]{1,2,0:T(8,128)S(1)}, f32[1,64,32]{1,2,0:T(8,128)S(1)}, u32[]{:S(2)}, u32[]{:S(2)}) collective-permute-start(f32[1,64,32]{1,2,0:T(8,128)S(1)} %fusion.40), channel_id=1, source_target_pairs={{0,4},{1,5},{2,6},{3,7},{4,8},{5,9},{6,10},{7,11},{8,12},{9,13},{1... | collective-permute-start | bytes 24584 | tf_op jit(solution)/shard_map/ppermute | solution.py:18
  79.5 9.1 %collective-permute-start.26 = (f32[1,64,32]{1,2,0:T(8,128)S(1)}, f32[1,64,32]{1,2,0:T(8,128)S(1)}, u32[]{:S(2)}, u32[]{:S(2)}) collective-permute-start(f32[1,64,32]{1,2,0:T(8,128)S(1)} %fusion.34), channel_id=1, source_target_pairs={{8,0},{9,1},{10,2},{11,3},{12,4},{13,5},{14,6},{15,7},{24,16},{25,... | collective-permute-start | bytes 24584 | tf_op jit(solution)/shard_map/ppermute | solution.py:18
  88.6 5.4 %collective-permute-start.25 = (f32[1,64,32]{1,2,0:T(8,128)S(1)}, f32[1,64,32]{1,2,0:T(8,128)S(1)}, u32[]{:S(2)}, u32[]{:S(2)}) collective-permute-start(f32[1,64,32]{1,2,0:T(8,128)S(1)} %fusion.34), channel_id=1, source_target_pairs={{0,8},{1,9},{2,10},{3,11},{4,12},{5,13},{6,14},{7,15},{16,24},{17,... | collective-permute-start | bytes 24584 | tf_op jit(solution)/shard_map/ppermute | solution.py:18
  94.8 5.4 %collective-permute-start.19 = (f32[1,64,32]{1,2,0:T(8,128)S(1)}, f32[1,64,32]{1,2,0:T(8,128)S(1)}, u32[]{:S(2)}, u32[]{:S(2)}) collective-permute-start(f32[1,64,32]{1,2,0:T(8,128)S(1)} %fusion.40), channel_id=1, source_target_pairs={{0,6},{1,7},{2,8},{3,9},{4,10},{5,11},{6,12},{7,13},{8,14},{9,15},... | collective-permute-start | bytes 24584 | tf_op jit(solution)/shard_map/ppermute | solution.py:18
  100.2 20.7 %collective-permute-start.9 = (f32[3,64,32]{1,2,0:T(8,128)S(1)}, f32[3,64,32]{1,2,0:T(8,128)S(1)}, u32[]{:S(2)}, u32[]{:S(2)}) collective-permute-start(f32[3,64,32]{1,2,0:T(8,128)S(1)} %copy-done.14), channel_id=1, source_target_pairs={{1,0},{2,1},{3,2},{4,3},{5,4},{6,5},{7,6},{8,7},{9,8},{10,9},{11,1... | collective-permute-start | bytes 73736 | tf_op jit(solution)/shard_map/ppermute | solution.py:18
  111.9 15.5 %collective-permute-start.8 = (f32[3,64,32]{1,2,0:T(8,128)S(1)}, f32[3,64,32]{1,2,0:T(8,128)S(1)}, u32[]{:S(2)}, u32[]{:S(2)}) collective-permute-start(f32[3,64,32]{1,2,0:T(8,128)S(1)} %copy-done.13), channel_id=1, source_target_pairs={{0,1},{1,2},{2,3},{3,4},{4,5},{5,6},{6,7},{7,8},{8,9},{9,10},{10,1... | collective-permute-start | bytes 73736 | tf_op jit(solution)/shard_map/ppermute | solution.py:18
  117.5 14.1 %collective-permute-start.7 = (f32[3,64,32]{1,2,0:T(8,128)S(1)}, f32[3,64,32]{1,2,0:T(8,128)S(1)}, u32[]{:S(2)}, u32[]{:S(2)}) collective-permute-start(f32[3,64,32]{1,2,0:T(8,128)S(1)} %copy-done.12), channel_id=1, source_target_pairs={{1,0},{2,1},{3,2},{4,3},{5,4},{6,5},{7,6},{8,7},{9,8},{10,9},{11,1... | collective-permute-start | bytes 73736 | tf_op jit(solution)/shard_map/ppermute | solution.py:18
  121.7 16.4 %collective-permute-start.6 = (f32[3,64,32]{1,2,0:T(8,128)S(1)}, f32[3,64,32]{1,2,0:T(8,128)S(1)}, u32[]{:S(2)}, u32[]{:S(2)}) collective-permute-start(f32[3,64,32]{1,2,0:T(8,128)S(1)} %copy-done.11), channel_id=1, source_target_pairs={{0,1},{1,2},{2,3},{3,4},{4,5},{5,6},{6,7},{7,8},{8,9},{9,10},{10,1... | collective-permute-start | bytes 73736 | tf_op jit(solution)/shard_map/ppermute | solution.py:18
  128.0 14.6 %collective-permute-start.5 = (f32[3,64,32]{1,2,0:T(8,128)S(1)}, f32[3,64,32]{1,2,0:T(8,128)S(1)}, u32[]{:S(2)}, u32[]{:S(2)}) collective-permute-start(f32[3,64,32]{1,2,0:T(8,128)S(1)} %copy-done.10), channel_id=1, source_target_pairs={{1,0},{2,1},{3,2},{4,3},{5,4},{6,5},{7,6},{8,7},{9,8},{10,9},{11,1... | collective-permute-start | bytes 73736 | tf_op jit(solution)/shard_map/ppermute | solution.py:18
  132.2 17.3 %collective-permute-start.4 = (f32[3,64,32]{1,2,0:T(8,128)S(1)}, f32[3,64,32]{1,2,0:T(8,128)S(1)}, u32[]{:S(2)}, u32[]{:S(2)}) collective-permute-start(f32[3,64,32]{1,2,0:T(8,128)S(1)} %copy-done.9), channel_id=1, source_target_pairs={{0,1},{1,2},{2,3},{3,4},{4,5},{5,6},{6,7},{7,8},{8,9},{9,10},{10,1... | collective-permute-start | bytes 73736 | tf_op jit(solution)/shard_map/ppermute | solution.py:18
  138.9 13.5 %collective-permute-start.3 = (f32[3,64,32]{1,2,0:T(8,128)S(1)}, f32[3,64,32]{1,2,0:T(8,128)S(1)}, u32[]{:S(2)}, u32[]{:S(2)}) collective-permute-start(f32[3,64,32]{1,2,0:T(8,128)S(1)} %copy-done.8), channel_id=1, source_target_pairs={{1,0},{2,1},{3,2},{4,3},{5,4},{6,5},{7,6},{8,7},{9,8},{10,9},{11,1... | collective-permute-start | bytes 73736 | tf_op jit(solution)/shard_map/ppermute | solution.py:18
  143.2 11.7 %collective-permute-start.2 = (f32[3,64,32]{1,2,0:T(8,128)S(1)}, f32[3,64,32]{1,2,0:T(8,128)S(1)}, u32[]{:S(2)}, u32[]{:S(2)}) collective-permute-start(f32[3,64,32]{1,2,0:T(8,128)S(1)} %copy-done.7), channel_id=1, source_target_pairs={{0,1},{1,2},{2,3},{3,4},{4,5},{5,6},{6,7},{7,8},{8,9},{9,10},{10,1... | collective-permute-start | bytes 73736 | tf_op jit(solution)/shard_map/ppermute | solution.py:18
  (37 other events, 107.3 us)
